TPU v7x, 32 devices: a whole 2x2x4 slice. The times are simulated.
32 devices in a mesh: elem: 8 (over z, y), col: 4 (over x, core).
Axes of the slice: x: 2, y: 2, z: 4, core: 2. Of those that a mesh axis runs over, the one named last changes fastest.
Arguments:
- gas: float32 [6, 93, 32768], P(None, None, ('elem', 'col')), may hold values from 0.01 to 0.3
- layer_mass: float32 [93, 32768], P(None, ('elem', 'col')), may hold values from 0.5 to 2
- solar_zenith_cosine: float32 [32768], P(('elem', 'col')), may hold values from 0.1 to 1
- albedo: float32 [32768], P(('elem', 'col')), may hold values from 0.05 to 0.6
- span_map: int32 [32768], P(('elem', 'col')), may hold values from 0 to 1023, as said below
- cloud: float32 [14, 93, 32768], P(None, None, ('elem', 'col')), may hold values from 0.001 to 0.03
- sunlit: int32 [32768], P(('elem', 'col')), may hold values from 0 to 1, as said below
- kabs: float32 [56, 6], replicated, may hold values from 0.002 to 0.02
- solar: float32 [56], replicated, may hold values from 0.1 to 1
Outputs:
- heating: float32 [93, 32768], P(None, ('elem', 'col'))
Inputs may be any that keep to these rules, and one draw needn't show every extreme that they name: `span_map`: within each device's 1024 consecutive entries the values are a permutation of 0 to 1023. 1 marks a sunlit column; the device at elem index e and the device at elem index e + 8 / 2 (modulo 8, same col index) hold exactly 1024 sunlit columns together, and in every draw some device has all of its 1024 columns sunlit.
All inputs are finite; a program needn't handle non-finite values.
Results may differ from a plain program's by a relative error of at most 0.0003.
Values sent between devices are 32-bit elements; how exact they have to be, the bound alone decides.
A program may use at most 128 MiB of HBM per device.

v0:
```python
import jax
import jax.numpy as jnp
from jax import lax
from jax.sharding import PartitionSpec as P

block_width = 128


def shortwave(absorber_block, cloud_block, mass_block, zenith, surface, kabs, solar):
    gpoints = kabs.shape[0]
    optical_thickness = jnp.einsum(
        "bw,wev->bev", kabs, absorber_block, precision=lax.Precision.HIGHEST
    )
    optical_thickness = optical_thickness + jnp.repeat(
        cloud_block, gpoints // cloud_block.shape[0], axis=0
    )
    depth = jnp.cumsum(optical_thickness, axis=1)
    depth = jnp.concatenate([jnp.zeros((gpoints, 1, depth.shape[2]), jnp.float32), depth], axis=1)
    down = solar[:, None, None] * zenith[None, None, :] * jnp.exp(-depth / zenith[None, None, :])
    total_depth = depth[:, -1:, :]
    upward = surface[None, None, :] * down[:, -1:, :] * jnp.exp(-1.66 * (total_depth - depth))
    net_flux = down - upward
    absorbed = jnp.sum(net_flux[:, :-1, :] - net_flux[:, 1:, :], axis=0)
    return absorbed / mass_block


def radiate(stacked, live_count, gas_count, level_count, band_count, kabs, solar):
    width = stacked.shape[1]
    summed_block = (live_count + block_width - 1) // block_width
    divided_absorbers = gas_count * level_count
    start_cloud = divided_absorbers + level_count + 2

    def step(block_index, output):
        start = block_index * block_width
        piece = lax.dynamic_slice_in_dim(stacked, start, block_width, 1)
        absorber_block = piece[:divided_absorbers].reshape(gas_count, level_count, block_width)
        mass_block = piece[divided_absorbers : divided_absorbers + level_count]
        zenith = piece[divided_absorbers + level_count]
        surface = piece[divided_absorbers + level_count + 1]
        cloud_block = piece[start_cloud:].reshape(band_count, level_count, block_width)
        rates = shortwave(absorber_block, cloud_block, mass_block, zenith, surface, kabs, solar)
        return lax.dynamic_update_slice_in_dim(output, rates, start, 1)

    empty = jnp.zeros((level_count, width), jnp.float32)
    return lax.fori_loop(0, summed_block, step, empty)


def on_device(gas, layer_mass, solar_zenith_cosine, albedo, span_map, cloud, sunlit, kabs, solar):
    gas_count, level_count, ncolumns = gas.shape
    band_count = cloud.shape[0]
    data = jnp.concatenate(
        [
            gas.reshape(gas_count * level_count, ncolumns),
            layer_mass,
            solar_zenith_cosine[None, :],
            albedo[None, :],
        ],
        axis=0,
    )
    slotted = jnp.zeros_like(data).at[:, span_map].set(data)
    physics = lax.all_to_all(slotted, ("elem", "col"), split_axis=1, concat_axis=1, tiled=True)
    stacked = jnp.concatenate([physics, cloud.reshape(band_count * level_count, ncolumns)], axis=0)
    live_count = jnp.sum(sunlit)
    column_index = jnp.arange(ncolumns, dtype=jnp.int32)
    lit_rank = jnp.cumsum(sunlit) - 1
    dark_rank = live_count + jnp.cumsum(1 - sunlit) - 1
    placement_index = jnp.where(sunlit == 1, lit_rank, dark_rank)
    order = jnp.zeros((ncolumns,), jnp.int32).at[placement_index].set(column_index)
    packed = stacked[:, order]
    padded = jnp.concatenate([packed, packed[:, : ncolumns // 2]], axis=1)
    rates = radiate(padded, live_count, gas_count, level_count, band_count, kabs, solar)
    valid = column_index[None, :] < live_count
    packed_rates = jnp.where(
        valid, rates[:, :ncolumns], jnp.zeros((level_count, ncolumns), jnp.float32)
    )
    physics_rates = jnp.zeros((level_count, ncolumns), jnp.float32).at[:, order].set(packed_rates)
    heating_rates_back = lax.all_to_all(
        physics_rates, ("elem", "col"), split_axis=1, concat_axis=1, tiled=True
    )
    return heating_rates_back[:, span_map]


def solution(mesh):
    in_specs = (
        P(None, None, ("elem", "col")),
        P(None, ("elem", "col")),
        P(("elem", "col")),
        P(("elem", "col")),
        P(("elem", "col")),
        P(None, None, ("elem", "col")),
        P(("elem", "col")),
        P(),
        P(),
    )
    out_specs = P(None, ("elem", "col"))
    return jax.shard_map(
        on_device, mesh=mesh, in_specs=in_specs, out_specs=out_specs, check_vma=False
    )
```

profile of v0, /device:TPU:0, one launch (start us, length us, event | category | flops | bytes accessed | tf_op | source)
XLA Modules:
  0.0 262.6 jit_solution(8308640911155611128)
XLA Ops:
  0.7 3.3 %reshape.96 = f32[558,1024]{1,0:T(8,128)} reshape(f32[6,93,1024]{2,1,0:T(8,128)} %param.11) | data formatting | bytes 4571136 | tf_op jit(solution)/shard_map/reshape | solution.py:53
  4.0 2.1 copy.19
  6.4 1.0 copy.21
  7.5 1.0 copy.22
  8.5 7.8 %scatter_custom_fusion.1 = f32[653,1024]{0,1:T(8,128)} fusion(s32[1024]{0:T(1024)S(1)} %get-tuple-element.68, f32[1,1024]{0,1:T(8,128)} %copy.22, f32[]{:T(128)} %constant.54, f32[1,1024]{0,1:T(8,128)} %copy.21, f32[93,1024]{0,1:T(8,128)S(1)} %copy.20, f32[558,1024]{0,1:T(8,128)S(1)} %copy.19, f32[]{:T(128)} %constant.43.clone.1), kind=kCustom, calls=%fused_computation.26 | custom fusion | flops 2006016 | bytes 5828616 | tf_op jit(solution)/shard_map/scatter | solution.py:60
  16.3 7.3 %all-to-all-start = ((f32[653,32,32]{0,2,1:T(8,128)}), f32[653,32,32]{0,2,1:T(8,128)S(1)}, u32[]{:S(2)}, u32[]{:S(2)}) async-start(f32[653,32,32]{0,2,1:T(8,128)} %bitcast.14), calls=%async_computation | async-start | bytes 6291456 | tf_op jit(solution)/shard_map/all_to_all | solution.py:61
  25.7 4.6 %reshape.97 = f32[1302,1024]{1,0:T(8,128)} reshape(f32[14,93,1024]{2,1,0:T(8,128)} %param.16) | data formatting | bytes 10665984 | tf_op jit(solution)/shard_map/reshape | solution.py:62
  30.3 6.2 %copy.23 = f32[1302,1024]{0,1:T(8,128)} copy(f32[1302,1024]{1,0:T(8,128)} %reshape.97) | data formatting | bytes 10665984 | tf_op jit(solution)/shard_map/reshape | solution.py:62
  37.4 4.3 %scatter_custom_fusion = s32[1024]{0:T(1024)S(1)} fusion(s32[1024]{0:T(1024)S(1)} %compare_select_fusion.2, s32[1024]{0:T(1024)S(1)} %iota.7, s32[]{:T(128)} %constant.44.clone.1), kind=kCustom, calls=%fused_computation.49 | custom fusion | bytes 4100 | tf_op jit(solution)/shard_map/scatter | solution.py:68
  42.4 52.7 %all-to-all-done = f32[653,32,32]{0,2,1:T(8,128)S(1)} async-done(((f32[653,32,32]{0,2,1:T(8,128)}), f32[653,32,32]{0,2,1:T(8,128)S(1)}, u32[]{:S(2)}, u32[]{:S(2)}) %all-to-all-start) | async-done | bytes 2674720 | tf_op jit(solution)/shard_map/all_to_all | solution.py:61
  95.1 7.7 %pad_maximum_fusion.1 = f32[1955,1024]{0,1:T(8,128)} fusion(f32[1302,1024]{0,1:T(8,128)} %copy.23, f32[653,1024]{0,1:T(8,128)S(1)} %bitcast.52), kind=kLoop, calls=%fused_computation.24 | loop fusion | flops 2001920 | bytes 16015360 | tf_op jit(solution)/shard_map/concatenate | solution.py:62
  102.8 12.5 %gather_fusion = f32[1024,1955]{1,0:T(8,128)} fusion(f32[1955,1024]{0,1:T(8,128)} %pad_maximum_fusion.1, s32[1024]{0:T(1024)S(1)} %get-tuple-element.69), kind=kCustom, calls=%fused_computation | custom fusion | bytes 16019456 | tf_op jit(solution)/shard_map/gather | solution.py:69
  115.2 2.6 slice.63
  117.8 2.0 copy-done.1
  119.9 7.2 %pad_maximum_fusion = f32[1955,1536]{0,1:T(8,128)} fusion(f32[1955,512]{0,1:T(8,128)S(1)} %slice.63, f32[1955,1024]{0,1:T(8,128)S(1)} %bitcast.50), kind=kLoop, calls=%fused_computation.23 | loop fusion | flops 3002880 | bytes 24023040 | tf_op jit(solution)/shard_map/concatenate | solution.py:70
  127.1 12.5 %copy.24 = f32[1955,1536]{1,0:T(8,128)} copy(f32[1955,1536]{0,1:T(8,128)} %pad_maximum_fusion) | data formatting | bytes 24023040 | tf_op jit(solution)/shard_map/while | solution.py:45
  139.6 48.7 %while.10 = (s32[]{:T(128)}, f32[93,1536]{1,0:T(8,128)S(1)}, s32[]{:T(128)}, f32[56]{0:T(128)S(1)}, f32[1955,1536]{1,0:T(8,128)}, /*index=5*/f32[56,6]{0,1:T(8,1...) while((s32[]{:T(128)}, f32[93,1536]{1,0:T(8,128)S(1)}, ...), condition=%wide.region_10.11_spmd, body=%wide.region_7.10_spmd.sunk | while | flops 118078472 | bytes 46607164 | solution.py:45
  139.8 1.0 constant_dynamic-slice_fusion.2
  140.8 3.8 %fusion.31 = f32[93,128,56]{1,2,0:T(8,128)} fusion(f32[6,93,128]{2,1,0:T(8,128)S(1)} %reshape.155, f32[56,6]{0,1:T(8,128)S(1)} %get-tuple-element.154), kind=kOutput, calls=%fused_computation.11.clone.1 | convolution fusion | flops 47996928 | bytes 2953536 | tf_op jit(solution)/shard_map/while/body/bw,wev->bev/dot_general | solution.py:11
  144.7 1.3 dynamic-slice.18
  152.0 1.0 constant_dynamic-slice_fusion.2
  153.0 3.8 %fusion.31 = f32[93,128,56]{1,2,0:T(8,128)} fusion(f32[6,93,128]{2,1,0:T(8,128)S(1)} %reshape.155, f32[56,6]{0,1:T(8,128)S(1)} %get-tuple-element.154), kind=kOutput, calls=%fused_computation.11.clone.1 | convolution fusion | flops 47996928 | bytes 2953536 | tf_op jit(solution)/shard_map/while/body/bw,wev->bev/dot_general | solution.py:11
  156.8 1.3 dynamic-slice.18
  164.1 1.0 constant_dynamic-slice_fusion.2
  165.1 3.8 %fusion.31 = f32[93,128,56]{1,2,0:T(8,128)} fusion(f32[6,93,128]{2,1,0:T(8,128)S(1)} %reshape.155, f32[56,6]{0,1:T(8,128)S(1)} %get-tuple-element.154), kind=kOutput, calls=%fused_computation.11.clone.1 | convolution fusion | flops 47996928 | bytes 2953536 | tf_op jit(solution)/shard_map/while/body/bw,wev->bev/dot_general | solution.py:11
  168.9 1.3 dynamic-slice.18
  176.2 1.0 constant_dynamic-slice_fusion.2
  177.2 3.8 %fusion.31 = f32[93,128,56]{1,2,0:T(8,128)} fusion(f32[6,93,128]{2,1,0:T(8,128)S(1)} %reshape.155, f32[56,6]{0,1:T(8,128)S(1)} %get-tuple-element.154), kind=kOutput, calls=%fused_computation.11.clone.1 | convolution fusion | flops 47996928 | bytes 2953536 | tf_op jit(solution)/shard_map/while/body/bw,wev->bev/dot_general | solution.py:11
  181.1 1.3 dynamic-slice.18
  188.6 3.8 %scatter_custom_fusion.2 = f32[93,1024]{0,1:T(8,128)S(1)} fusion(s32[1024]{0:T(1024)S(1)} %get-tuple-element.70, f32[93,1536]{0,1:T(8,128)S(1)} %copy.25, f32[]{:T(128)} %constant.43.clone.1, pred[1024]{0:T(1024)(128)(4,1)S(1)} %iota_compare_fusion), kind=kCustom, calls=%fused_computation.36 | custom fusion | flops 95232 | bytes 907264 | tf_op jit(solution)/shard_map/scatter | solution.py:76
  192.4 66.4 %all_to_all.24 = f32[93,32,32]{0,2,1:T(8,128)S(1)} all-to-all(f32[93,32,32]{0,2,1:T(8,128)S(1)} %bitcast.53), channel_id=1, replica_groups=mesh['elem'=8,'col'=4] {'elem','col'}, dimensions={1} | all-to-all | bytes 761856 | tf_op jit(solution)/shard_map/all_to_all | solution.py:77
  258.8 2.8 %gather_fusion.1 = f32[1024,93]{1,0:T(8,128)S(1)} fusion(f32[93,1024]{0,1:T(8,128)S(1)} %bitcast.51, s32[1024]{0:T(1024)S(1)} %get-tuple-element.67), kind=kCustom, calls=%fused_computation.1 | custom fusion | bytes 765952 | tf_op jit(solution)/shard_map/gather | solution.py:80
  (86 shorter events, 28.7 us)
Async XLA Ops:
  4.0 2.2 copy-start.2
  4.0 2.4 copy-start.6
  4.0 3.4 %copy-start.7 = (f32[1024]{0:T(1024)S(1)}, f32[1024]{0:T(1024)}, u32[]{:S(2)}) copy-start(f32[1024]{0:T(1024)} %param.14) | copy-start | bytes 12292
  16.3 7.3 %copy-start.4 = (s32[1024]{0:T(1024)S(1)}, s32[1024]{0:T(1024)}, u32[]{:S(2)}) copy-start(s32[1024]{0:T(1024)} %param.17) | copy-start | bytes 12292
  16.3 78.8 %all-to-all-start = ((f32[653,32,32]{0,2,1:T(8,128)}), f32[653,32,32]{0,2,1:T(8,128)S(1)}, u32[]{:S(2)}, u32[]{:S(2)}) async-start(f32[653,32,32]{0,2,1:T(8,128)} %bitcast.14), calls=%async_computation | async-start | bytes 6291456 | tf_op jit(solution)/shard_map/all_to_all | solution.py:61
  115.2 4.6 %copy-start.1 = (f32[1024,1955]{1,0:T(8,128)S(1)}, f32[1024,1955]{1,0:T(8,128)}, u32[]{:S(2)}) copy-start(f32[1024,1955]{1,0:T(8,128)} %gather_fusion) | copy-start | bytes 24023044
  127.1 12.5 %copy-start.3 = (f32[56,6]{0,1:T(8,128)S(1)}, f32[56,6]{0,1:T(8,128)}, u32[]{:S(2)}) copy-start(f32[56,6]{0,1:T(8,128)} %param.18) | copy-start | bytes 4036
  127.1 12.5 %copy-start.5 = (f32[56]{0:T(128)S(1)}, f32[56]{0:T(128)}, u32[]{:S(2)}) copy-start(f32[56]{0:T(128)} %param.19) | copy-start | bytes 676
  146.1 1.8 copy-start
  158.2 1.8 copy-start
  170.3 1.8 copy-start
  182.4 1.8 copy-start
where the time goes:
time: 265 us; the launch traced here: 263 us
  local copies, waits for them, and re-layouts  76.6 us (29%)
  blocking collectives  66.4 us (25%)
  waiting for transfers between devices  52.7 us (20%)
  other arithmetic  42.9 us (16%)
  matrix products  15.3 us (6%)
  starting transfers between devices  7.3 us (3%)
    all_to_all x1, blocking collectives, on_device(): lax.all_to_all(physics_rates, ('elem', 'col'), split_axis=1, concat_axis=...  66.4 us
    all_to_all x1, waiting for transfers between devices, on_device(): lax.all_to_all(slotted, ('elem', 'col'), split_axis=1, concat_axis=1, til...  52.7 us
    dot_general x4, matrix products, shortwave(): jnp.einsum('bw,wev->bev', kabs, absorber_block, precision=lax.Precision.H...  15.3 us
    while x2, local copies, waits for them, and re-layouts, radiate(): return lax.fori_loop(0, summed_block, step, empty)  12.7 us
    gather x1, local copies, waits for them, and re-layouts, on_device(): packed = stacked[:, order]  12.5 us
    reshape x2, local copies, waits for them, and re-layouts, on_device(): cloud.reshape(band_count * level_count, ncolumns)  10.8 us
    scatter x1, other arithmetic, on_device(): slotted = jnp.zeros_like(data).at[:, span_map].set(data)  7.84 us
    concatenate x1, other arithmetic, on_device(): jnp.concatenate([physics, cloud.reshape(band_count * level_count, ncolumn...  7.69 us
  transfers between devices with their start and end apart: 1, of which 1 were waited for; matrix products, arithmetic and copies ran while one was open for 7% of the time, Pallas kernels for 0%

commit v1 on v0

v1 whole, which is shorter than its diff:
```python
import functools

import jax
import jax.numpy as jnp
from jax import lax
from jax.experimental import pallas as pl
from jax.experimental.pallas import tpu as pltpu
from jax.sharding import PartitionSpec as P

MESH = pl.DeviceIdType.MESH
LANES = 128
LOG2E = 1.4426950408889634


def flip(a, b, size):
    out, bit = 0, 1
    while bit < size:
        out = out + lax.rem(lax.div(a, bit) + lax.div(b, bit), 2) * bit
        bit *= 2
    return out


def swap_blocks(rows, blocks, slots):
    lane = lax.broadcasted_iota(jnp.int32, rows[0].shape, 1) // slots
    out = []
    for b in range(blocks):
        piece = None
        for a in range(blocks):
            shift = (a - b) * slots % LANES
            moved = pltpu.roll(rows[a], shift, 1) if shift else rows[a]
            piece = moved if piece is None else jnp.where(lane == a, moved, piece)
        out.append(piece)
    return out


def split_two(x):
    high = x.astype(jnp.bfloat16)
    return high, (x - high.astype(jnp.float32)).astype(jnp.bfloat16)


def fused_kernel(
    sizes,
    gas_hbm, cloud_hbm, zenith_ref, albedo_ref, span_ref, lit_ref, kabs_ref, solar_ref,
    out_ref,
    gas_v, cloud_v, high_v, low_v, onehot, sends, recvs, stack, cums, rates_out, rates_in, total,
    gas_sem, cloud_sem, send_sem, recv_sem, rate_send_sem, rate_recv_sem,
):
    gases, levels, bands, per_band, devices, cols, slots, part, send_order, work_order = sizes
    blocks = LANES // slots
    full = part * blocks
    tiles = devices // blocks
    width = tiles * LANES
    me = lax.axis_index("elem") * cols + lax.axis_index("col")
    mine, place = lax.div(me, blocks), lax.rem(me, blocks)

    def at(device):
        return (lax.div(device, cols), lax.rem(device, cols))

    gas_copy = pltpu.make_async_copy(gas_hbm, gas_v, gas_sem)
    gas_copy.start()
    cloud_copy = pltpu.make_async_copy(cloud_hbm, cloud_v, cloud_sem)
    cloud_copy.start()

    barrier = pltpu.get_barrier_semaphore()

    def greet(k, carry):
        other = lax.rem(me + k, devices)
        pl.semaphore_signal(
            barrier, inc=1, device_id=at(other), device_id_type=MESH
        )
        return carry

    lax.fori_loop(1, devices, greet, 0)

    def hot(q, carry):
        first = pl.multiple_of(q * LANES, LANES)
        slot = lax.broadcasted_iota(jnp.int32, (LANES, width), 0) + first
        onehot[pl.ds(first, LANES), :] = (slot == span_ref[...]).astype(jnp.float32).astype(jnp.bfloat16)
        return carry

    lax.fori_loop(0, tiles, hot, 0)
    gas_copy.wait()
    for s in range(gases):
        if s == 0:
            tail = [zenith_ref[...], albedo_ref[...], jnp.zeros((full - levels - 2, width), jnp.float32)]
        else:
            tail = [jnp.zeros((full - levels, width), jnp.float32)]
        high, low = split_two(jnp.concatenate([gas_v[s]] + tail, axis=0))
        high_v[s * full : (s + 1) * full, :] = high
        low_v[s * full : (s + 1) * full, :] = low
    pl.semaphore_wait(barrier, devices - 1)

    def state_copy(src, dst, device, sent, came):
        return pltpu.make_async_remote_copy(
            sends.at[src], recvs.at[dst], send_sem.at[sent], recv_sem.at[came],
            device_id=at(device), device_id_type=MESH,
        )

    def rate_copy(src, dst, device, sent, came):
        return pltpu.make_async_remote_copy(
            rates_out.at[src], rates_in.at[dst], rate_send_sem.at[sent], rate_recv_sem.at[came],
            device_id=at(device), device_id_type=MESH,
        )

    def send_tile(k, carry):
        turn = send_order(k)
        q = flip(mine, turn, tiles)
        hot_q = onehot[pl.ds(pl.multiple_of(q * LANES, LANES), LANES), :]
        dims = (((1,), (1,)), ((), ()))
        slotted = lax.dot_general(high_v[...], hot_q, dims, preferred_element_type=jnp.float32)
        slotted = slotted + lax.dot_general(low_v[...], hot_q, dims, preferred_element_type=jnp.float32)
        for s in range(gases):
            rows = [slotted[s * full + j * part : s * full + (j + 1) * part] for j in range(blocks)]
            for t, piece in enumerate(swap_blocks(rows, blocks, slots)):
                sends[q * blocks + t, s * part : (s + 1) * part, :] = piece
        for step in range(blocks):
            t = lax.rem(place + step, blocks)
            to = q * blocks + t

            @pl.when(to != me)
            def _():
                state_copy(to, me, to, to, me).start()

            @pl.when(to == me)
            def _():
                recvs[me] = sends[me]

        return carry

    lax.fori_loop(0, tiles, send_tile, 0)

    stack[levels:full, :] = jnp.zeros((full - levels, stack.shape[1]), jnp.float32)
    upper = lax.broadcasted_iota(jnp.int32, (full, full), 0)
    lower = lax.broadcasted_iota(jnp.int32, (full, full), 1)
    above = (lower < upper).astype(jnp.float32).astype(jnp.bfloat16)
    cloud_copy.wait()

    def work_tile(k, carry):
        turn = work_order(k)
        q = flip(mine, turn, tiles)
        lanes = pl.ds(pl.multiple_of(q * LANES, LANES), LANES)
        for b in range(bands):
            stack[0:levels, (gases + b) * LANES : (gases + b + 1) * LANES] = cloud_v[b, :, lanes]
        for t in range(blocks):
            source = q * blocks + t

            @pl.when(source != me)
            def _():
                state_copy(source, source, source, source, source).wait_recv()

        zenith = surface = None
        for s in range(gases):
            rows = [recvs[q * blocks + t, s * part : (s + 1) * part, :] for t in range(blocks)]
            pieces = swap_blocks(rows, blocks, slots)
            for j, piece in enumerate(pieces):
                keep = max(0, min(part, levels - j * part))
                if keep == 0:
                    continue
                stack[j * part : j * part + keep, s * LANES : (s + 1) * LANES] = piece[0:keep]
            if s == 0:
                row = levels % part
                zenith = pieces[levels // part][row : row + 1]
                row = (levels + 1) % part
                surface = pieces[(levels + 1) // part][row : row + 1]
        for f in range(gases + bands):
            high, low = split_two(stack[:, f * LANES : (f + 1) * LANES])
            cums[f] = jnp.dot(above, high, preferred_element_type=jnp.float32) + jnp.dot(
                above, low, preferred_element_type=jnp.float32
            )
        slant = -LOG2E / zenith

        def band(b, net):
            clouds = cums[gases + b]
            for i in range(per_band):
                g = b * per_band + i
                depth = clouds
                for s in range(gases):
                    depth = depth + kabs_ref[g * gases + s] * cums[s]
                down = jnp.exp2(depth * slant)
                up = jnp.exp2((depth - depth[levels : levels + 1]) * (1.66 * LOG2E))
                net = net + solar_ref[g] * (down - (surface * down[levels : levels + 1]) * up)
            return net

        net = lax.fori_loop(0, bands, band, jnp.zeros((full, LANES), jnp.float32))
        absorbed = (net - pltpu.roll(net, full - 1, 0)) * zenith
        absorbed = jnp.where(lit_ref[:, lanes] == 1, absorbed, jnp.zeros_like(absorbed))
        rows = [absorbed[j * part : (j + 1) * part] for j in range(blocks)]
        for t, piece in enumerate(swap_blocks(rows, blocks, slots)):
            rates_out[q * blocks + t] = piece
        for t in range(blocks):
            to = q * blocks + t

            @pl.when(to != me)
            def _():
                rate_copy(to, me, to, to, me).start()

            @pl.when(to == me)
            def _():
                rates_in[me] = rates_out[me]

        return carry

    lax.fori_loop(0, tiles, work_tile, 0)

    total[...] = jnp.zeros_like(total)

    def gather_tile(k, carry):
        q = flip(mine, work_order(k), tiles)
        for t in range(blocks):
            source = q * blocks + t

            @pl.when(source != me)
            def _():
                rate_copy(source, source, source, source, source).wait_recv()

        rows = [rates_in[q * blocks + t] for t in range(blocks)]
        high, low = split_two(jnp.concatenate(swap_blocks(rows, blocks, slots), axis=0))
        hot_q = onehot[pl.ds(pl.multiple_of(q * LANES, LANES), LANES), :]
        total[...] += jnp.dot(high, hot_q, preferred_element_type=jnp.float32) + jnp.dot(
            low, hot_q, preferred_element_type=jnp.float32
        )
        return carry

    lax.fori_loop(0, tiles, gather_tile, 0)
    out_ref[...] = total[0:levels, :]

    def drain(k, carry):
        other = lax.rem(me + k, devices)
        state_copy(other, me, other, other, me).wait_send()
        rate_copy(other, me, other, other, me).wait_send()
        return carry

    lax.fori_loop(1, devices, drain, 0)


def send_order(k):
    return lax.rem(k + 4, 8)


def work_order(k):
    return k


def fused(elems, cols, gas, layer_mass, solar_zenith_cosine, albedo, span_map, cloud, sunlit, kabs, solar):
    gases, levels, width = gas.shape
    bands = cloud.shape[0]
    gpoints = kabs.shape[0]
    devices = elems * cols
    slots = width // devices
    blocks = LANES // slots
    part = -(-(levels + 2) // (8 * blocks)) * 8
    full = part * blocks
    sizes = (gases, levels, bands, gpoints // bands, devices, cols, slots, part, send_order, work_order)
    vmem = pl.BlockSpec(memory_space=pltpu.VMEM)
    smem = pl.BlockSpec(memory_space=pltpu.SMEM)
    hbm = pl.BlockSpec(memory_space=pl.ANY)
    f32, bf16 = jnp.float32, jnp.bfloat16
    absorbed = pl.pallas_call(
        functools.partial(fused_kernel, sizes),
        out_shape=jax.ShapeDtypeStruct((levels, width), f32),
        in_specs=[hbm, hbm, vmem, vmem, vmem, vmem, smem, smem],
        out_specs=vmem,
        scratch_shapes=[
            pltpu.VMEM((gases, levels, width), f32),
            pltpu.VMEM((bands, levels, width), f32),
            pltpu.VMEM((gases * full, width), bf16),
            pltpu.VMEM((gases * full, width), bf16),
            pltpu.VMEM((width, width), bf16),
            pltpu.VMEM((devices, gases * part, LANES), f32),
            pltpu.VMEM((devices, gases * part, LANES), f32),
            pltpu.VMEM((full, (gases + bands) * LANES), f32),
            pltpu.VMEM((gases + bands, full, LANES), f32),
            pltpu.VMEM((devices, part, LANES), f32),
            pltpu.VMEM((devices, part, LANES), f32),
            pltpu.VMEM((full, width), f32),
            pltpu.SemaphoreType.DMA,
            pltpu.SemaphoreType.DMA,
            pltpu.SemaphoreType.DMA((devices,)),
            pltpu.SemaphoreType.DMA((devices,)),
            pltpu.SemaphoreType.DMA((devices,)),
            pltpu.SemaphoreType.DMA((devices,)),
        ],
        compiler_params=pltpu.CompilerParams(
            collective_id=0, has_side_effects=True, vmem_limit_bytes=40 * 1024 * 1024
        ),
        name="remap_and_radiate",
    )(
        gas, cloud, solar_zenith_cosine[None, :], albedo[None, :], span_map[None, :], sunlit[None, :],
        kabs.reshape(-1), solar,
    )
    return absorbed / layer_mass


def solution(mesh):
    in_specs = (
        P(None, None, ("elem", "col")),
        P(None, ("elem", "col")),
        P(("elem", "col")),
        P(("elem", "col")),
        P(("elem", "col")),
        P(None, None, ("elem", "col")),
        P(("elem", "col")),
        P(),
        P(),
    )
    out_specs = P(None, ("elem", "col"))
    body = functools.partial(fused, mesh.shape["elem"], mesh.shape["col"])
    return jax.shard_map(
        body, mesh=mesh, in_specs=in_specs, out_specs=out_specs, check_vma=False
    )
```

time: 265 us -> 84.5 us (0.32)
  Pallas kernels: 0 us -> 74.8 us
  local copies, waits for them, and re-layouts: 76.6 us -> 8.53 us
  blocking collectives: 66.4 us -> 0 us
  waiting for transfers between devices: 52.7 us -> 0 us
  other arithmetic: 42.9 us -> 0.82 us
  matrix products: 15.3 us -> 0 us
  starting transfers between devices: 7.3 us -> 0 us
    pallas_call x0 -> x1, Pallas kernels: none -> 74.8 us  [fused(): pl.pallas_call(functools.partial(fused_kernel, sizes), out_shape=jax.Shap...]
    all_to_all x1 -> x0, blocking collectives: 66.4 us -> none  [on_device(): lax.all_to_all(physics_rates, ('elem', 'col'), split_axis=1, concat_axis=...]
    all_to_all x1 -> x0, waiting for transfers between devices: 52.7 us -> none  [on_device(): lax.all_to_all(slotted, ('elem', 'col'), split_axis=1, concat_axis=1, til...]
    reshape x16 -> x1, local copies, waits for them, and re-layouts: 18.1 us -> 0.13 us  [fused(): kabs.reshape(-1)]
    while x10 -> x0, local copies, waits for them, and re-layouts: 16.3 us -> none  [the longest x2 12.7 us: radiate(): return lax.fori_loop(0, summed_block, step, empty)]
    gather x3 -> x0, local copies, waits for them, and re-layouts: 16.2 us -> none  [the longest x1 12.5 us: on_device(): packed = stacked[:, order]]
    dot_general x4 -> x0, matrix products: 15.3 us -> none  [shortwave(): jnp.einsum('bw,wev->bev', kabs, absorber_block, precision=lax.Precision.H...]
    concatenate x2 -> x0, other arithmetic: 14.9 us -> none  [the longest x1 7.69 us: on_device(): jnp.concatenate([physics, cloud.reshape(band_count * level_count, ncolumn...]
  transfers between devices with their start and end apart: 1 -> 0, of which waited for: 1 -> 0; matrix products, arithmetic and copies ran while one was open for 7% -> 0% of each run, Pallas kernels for 0% -> 0%
where the time goes in v1:
time: 84.5 us; the launch traced here: 84.2 us
  Pallas kernels  74.8 us (89%)
  local copies, waits for them, and re-layouts  8.53 us (10%)
    pallas_call x1, Pallas kernels, fused(): pl.pallas_call(functools.partial(fused_kernel, sizes), out_shape=jax.Shap...  74.8 us
    unnamed x17, local copies, waits for them, and re-layouts  8.4 us

profile of v1, /device:TPU:0, one launch (start us, length us, event | category | flops | bytes accessed | tf_op | source)
XLA Modules:
  0.0 84.2 jit_solution(14601282552999046424)
XLA Ops:
  0.0 0.8 copy.10
  0.8 0.1 reshape.3.kabs_ref
  0.9 0.0 copy-start
  0.9 2.6 %copy-done = f32[14,93,1024]{2,1,0:T(8,128)S(1)} copy-done((f32[14,93,1024]{2,1,0:T(8,128)S(1)}, f32[14,93,1024]{2,1,0:T(8,128)}, u32[]{:S(2)}) %copy-start) | copy-done | bytes 5333016
  3.5 0.0 copy-start.1
  3.5 1.7 %copy-done.1 = f32[6,93,1024]{2,1,0:T(8,128)S(1)} copy-done((f32[6,93,1024]{2,1,0:T(8,128)S(1)}, f32[6,93,1024]{2,1,0:T(8,128)}, u32[]{:S(2)}) %copy-start.1) | copy-done | bytes 2285592
  5.1 0.0 copy-start.2
  5.1 0.7 copy-done.2
  5.8 0.0 copy-start.3
  5.8 0.7 copy-done.3
  6.5 0.0 copy-start.4
  6.5 0.7 copy-done.4
  7.2 0.0 copy-start.5
  7.2 0.7 copy-done.5
  7.9 0.0 copy-start.6
  7.9 0.7 copy-done.6
  8.5 0.0 copy-start.7
  8.5 74.8 %remap_and_radiate.1 = f32[93,1024]{1,0:T(8,128)S(1)} custom-call(f32[6,93,1024]{2,1,0:T(8,128)S(1)} %copy-done.1, f32[14,93,1024]{2,1,0:T(8,128)S(1)} %copy-done, f32[1,1024]{1,0:T(1,128)S(1)} %bitcast.4, f32[1,1024]{1,0:T(1,128)S(1)} %bitcast.5, s32[1,1024]{1,0:T(1,128)S(1)} %bitcast.6, s32[1,1024]{1,0:T(1,128)S(1)} %bitcast.7, f32[336]{0:T(512)S(1)} %reshape.3.kabs_ref, ...), custom_call_target="tpu_custom_call" | custom-call | tf_op jit(solution)/shard_map/remap_and_radiate/pallas_call | solution.py:258
  83.3 0.0 copy-done.7
  83.4 0.8 div.3
Async XLA Ops:
  0.9 2.6 %copy-start = (f32[14,93,1024]{2,1,0:T(8,128)S(1)}, f32[14,93,1024]{2,1,0:T(8,128)}, u32[]{:S(2)}) copy-start(f32[14,93,1024]{2,1,0:T(8,128)} %cloud_hbm.1) | copy-start | bytes 15998980
  3.5 1.7 %copy-start.1 = (f32[6,93,1024]{2,1,0:T(8,128)S(1)}, f32[6,93,1024]{2,1,0:T(8,128)}, u32[]{:S(2)}) copy-start(f32[6,93,1024]{2,1,0:T(8,128)} %gas_hbm.1) | copy-start | bytes 6856708
  5.1 0.7 copy-start.2
  5.8 0.7 copy-start.3
  6.5 0.7 copy-start.4
  7.2 0.7 copy-start.5
  7.9 0.7 copy-start.6
  8.5 74.8 %copy-start.7 = (f32[93,1024]{1,0:T(8,128)S(1)}, f32[93,1024]{1,0:T(8,128)}, u32[]{:S(2)}) copy-start(f32[93,1024]{1,0:T(8,128)} %param.10) | copy-start | bytes 1142788

commit v2 on v1

--- a/solution.py
+++ b/solution.py
@@ -134,6 +134,25 @@
     lower = lax.broadcasted_iota(jnp.int32, (full, full), 1)
     above = (lower < upper).astype(jnp.float32).astype(jnp.bfloat16)
     cloud_copy.wait()
+
+    total[...] = jnp.zeros_like(total)
+
+    def gather_tile(k, carry):
+        q = flip(mine, work_order(k), tiles)
+        for t in range(blocks):
+            source = q * blocks + t
+
+            @pl.when(source != me)
+            def _():
+                rate_copy(source, source, source, source, source).wait_recv()
+
+        rows = [rates_in[q * blocks + t] for t in range(blocks)]
+        high, low = split_two(jnp.concatenate(swap_blocks(rows, blocks, slots), axis=0))
+        hot_q = onehot[pl.ds(pl.multiple_of(q * LANES, LANES), LANES), :]
+        total[...] += jnp.dot(high, hot_q, preferred_element_type=jnp.float32) + jnp.dot(
+            low, hot_q, preferred_element_type=jnp.float32
+        )
+        return carry
 
     def work_tile(k, carry):
         turn = work_order(k)
@@ -164,10 +183,11 @@
                 surface = pieces[(levels + 1) // part][row : row + 1]
         for f in range(gases + bands):
             high, low = split_two(stack[:, f * LANES : (f + 1) * LANES])
-            cums[f] = jnp.dot(above, high, preferred_element_type=jnp.float32) + jnp.dot(
+            summed = jnp.dot(above, high, preferred_element_type=jnp.float32) + jnp.dot(
                 above, low, preferred_element_type=jnp.float32
             )
-        slant = -LOG2E / zenith
+            cums[f] = summed * (1.66 * LOG2E)
+        slant = -1.0 / (1.66 * zenith)
 
         def band(b, net):
             clouds = cums[gases + b]
@@ -177,8 +197,9 @@
                 for s in range(gases):
                     depth = depth + kabs_ref[g * gases + s] * cums[s]
                 down = jnp.exp2(depth * slant)
-                up = jnp.exp2((depth - depth[levels : levels + 1]) * (1.66 * LOG2E))
-                net = net + solar_ref[g] * (down - (surface * down[levels : levels + 1]) * up)
+                up = jnp.exp2(depth)
+                back = surface * down[levels : levels + 1] * jnp.exp2(-depth[levels : levels + 1])
+                net = net + solar_ref[g] * (down - back * up)
             return net
 
         net = lax.fori_loop(0, bands, band, jnp.zeros((full, LANES), jnp.float32))
@@ -201,26 +222,6 @@
         return carry
 
     lax.fori_loop(0, tiles, work_tile, 0)
-
-    total[...] = jnp.zeros_like(total)
-
-    def gather_tile(k, carry):
-        q = flip(mine, work_order(k), tiles)
-        for t in range(blocks):
-            source = q * blocks + t
-
-            @pl.when(source != me)
-            def _():
-                rate_copy(source, source, source, source, source).wait_recv()
-
-        rows = [rates_in[q * blocks + t] for t in range(blocks)]
-        high, low = split_two(jnp.concatenate(swap_blocks(rows, blocks, slots), axis=0))
-        hot_q = onehot[pl.ds(pl.multiple_of(q * LANES, LANES), LANES), :]
-        total[...] += jnp.dot(high, hot_q, preferred_element_type=jnp.float32) + jnp.dot(
-            low, hot_q, preferred_element_type=jnp.float32
-        )
-        return carry
-
     lax.fori_loop(0, tiles, gather_tile, 0)
     out_ref[...] = total[0:levels, :]
 
@@ -234,11 +235,11 @@
 
 
 def send_order(k):
-    return lax.rem(k + 4, 8)
+    return lax.rem(k + 1, 2) * 4 + lax.div(k, 2)
 
 
 def work_order(k):
-    return k
+    return lax.rem(k, 2) * 4 + lax.div(k, 2)
 
 
 def fused(elems, cols, gas, layer_mass, solar_zenith_cosine, albedo, span_map, cloud, sunlit, kabs, solar):
@@ -253,7 +254,7 @@
     sizes = (gases, levels, bands, gpoints // bands, devices, cols, slots, part, send_order, work_order)
     vmem = pl.BlockSpec(memory_space=pltpu.VMEM)
     smem = pl.BlockSpec(memory_space=pltpu.SMEM)
-    hbm = pl.BlockSpec(memory_space=pl.ANY)
+    hbm = pl.BlockSpec(memory_space=pltpu.HBM)
     f32, bf16 = jnp.float32, jnp.bfloat16
     absorbed = pl.pallas_call(
         functools.partial(fused_kernel, sizes),
@@ -281,7 +282,7 @@
             pltpu.SemaphoreType.DMA((devices,)),
         ],
         compiler_params=pltpu.CompilerParams(
-            collective_id=0, has_side_effects=True, vmem_limit_bytes=40 * 1024 * 1024
+            collective_id=0, has_side_effects=True, vmem_limit_bytes=62 * 1024 * 1024
         ),
         name="remap_and_radiate",
     )(

time: 84.5 us -> 75.8 us (0.90); the launches traced: 84.2 us -> 74.4 us
  local copies, waits for them, and re-layouts: 8.53 us -> 1.54 us
  Pallas kernels: 74.8 us -> 71.1 us
  other arithmetic: 0.82 us -> 1.8 us
    unnamed x17 -> x3, local copies, waits for them, and re-layouts: 8.4 us -> 0.83 us
    pallas_call x1, Pallas kernels: 74.8 us -> 71.1 us  [fused(): pl.pallas_call(functools.partial(fused_kernel, sizes), out_shape=jax.Shap...]
    div x1, other arithmetic: 0.82 us -> 1.8 us  [fused(): return absorbed / layer_mass]
where the time goes in v2:
time: 75.8 us; the launch traced here: 74.4 us
  Pallas kernels  71.1 us (94%)
  other arithmetic  1.8 us (2%)
  local copies, waits for them, and re-layouts  1.54 us (2%)
    pallas_call x1, Pallas kernels, fused(): pl.pallas_call(functools.partial(fused_kernel, sizes), out_shape=jax.Shap...  71.1 us
    div x1, other arithmetic, fused(): return absorbed / layer_mass  1.8 us

profile of v2, /device:TPU:0, one launch (start us, length us, event | category | flops | bytes accessed | tf_op | source)
XLA Modules:
  0.0 74.4 jit_solution(14549962382163165116)
XLA Ops:
  0.0 0.0 copy-start
  0.0 0.8 %copy.10 = f32[56,6]{1,0:T(8,128)S(1)} copy(f32[56,6]{0,1:T(8,128)} %param.16) | data formatting | bytes 2688 | tf_op args[7]
  0.8 0.7 reshape.3.kabs_ref
  1.5 71.1 %remap_and_radiate.1 = f32[93,1024]{1,0:T(8,128)} custom-call(f32[6,93,1024]{2,1,0:T(8,128)} %gas_hbm.1, f32[14,93,1024]{2,1,0:T(8,128)} %cloud_hbm.1, f32[1,1024]{1,0:T(1,128)} %bitcast.4, f32[1,1024]{1,0:T(1,128)} %bitcast.5, s32[1,1024]{1,0:T(1,128)} %bitcast.6, s32[1,1024]{1,0:T(1,128)} %bitcast.7, f32[336]{0:T(512)} %reshape.3.kabs_ref, f32[56]{0:T(128)} %solar_ref.1), custom_call_target="tpu_custom_call" | custom-call | tf_op jit(solution)/shard_map/remap_and_radiate/pallas_call | solution.py:259
  72.6 0.0 copy-done
  72.6 1.8 %div.3 = f32[93,1024]{1,0:T(8,128)} divide(f32[93,1024]{1,0:T(8,128)} %remap_and_radiate.1, f32[93,1024]{1,0:T(8,128)S(1)} %copy-done) | non-fusion elementwise | flops 95232 | bytes 1142784 | tf_op jit(solution)/shard_map/div | solution.py:292
Async XLA Ops:
  0.0 72.6 %copy-start = (f32[93,1024]{1,0:T(8,128)S(1)}, f32[93,1024]{1,0:T(8,128)}, u32[]{:S(2)}) copy-start(f32[93,1024]{1,0:T(8,128)} %param.10) | copy-start | bytes 1142788
